TPU v7x, 128 devices: a whole 4x4x4 slice. The times are simulated.
128 devices in a mesh: expert: 8 (over z, core), fsdp: 16 (over y, x).
Axes of the slice: x: 4, y: 4, z: 4, core: 2. Of those that a mesh axis runs over, the one named last changes fastest.
Arguments:
- gradient: bfloat16 [16, 7168, 2048], P('expert', 'fsdp'), may hold values from -6 to 6
- momentum: float32 [16, 7168, 2048], P('expert', 'fsdp'), may hold values from -6 to 6
- right_factor: float32 [16, 2048, 128], P('expert'), may hold values from -6 to 6
- placement: int32 [16], replicated, may hold values from 0 to 15, as said below
Outputs:
- new_momentum: float32 [16, 7168, 2048], P('expert', 'fsdp')
- new_right: float32 [16, 2048, 128], P('expert')
- left_at_owner: bfloat16 [16, 7168, 128], P('expert', 'fsdp')
- right_at_owner: bfloat16 [16, 2048, 128], P('expert', 'fsdp')
Inputs may be any that keep to these rules, and one draw needn't show every extreme that they name: placement names each serving slot once; slot s belongs to index s // 2 of expert; expert 2i+j (j = 0, 1) is served on index (i+1) % 8 of expert if j = 0 and on index (i+4) % 8 if j = 1; which of that index's 2 slots it takes is not fixed.
All inputs are finite; a program needn't handle non-finite values.
Results may differ from a plain program's by a relative error of at most 0.001.
Values may be sent and summed in bfloat16 or wider, within the bound.
A program may use at most 128 MiB of HBM per device.

v0:
```python
import functools
import math

import jax
import jax.numpy as jnp
from jax import lax
from jax.experimental import pallas as pl
from jax.experimental.pallas import tpu as pltpu
from jax.sharding import PartitionSpec as P

D = 7168
FEEDBACK = 0.05
EPSILON = 1e-06

EXPERTS_HERE = 2
ROWS = 448
FF = 2048
RANK = 128
SIDE = 4
PEERS = SIDE * SIDE
GROUPS = 8
PARTS = 2
PART_ROWS = ROWS // PARTS
BLOCK = 8
HEAD = 16
TILE = RANK + HEAD
CHUNK = SIDE * RANK + HEAD
MESH = pl.DeviceIdType.MESH
F32 = jnp.float32
BF16 = jnp.bfloat16
CODE = jnp.int16


def split(value):
    high = value.astype(BF16)
    return high, (value - high.astype(F32)).astype(BF16)


def dot(a, b):
    return jnp.dot(a, b, preferred_element_type=F32)


def dot_last(a, b):
    return lax.dot_general(a, b, (((1,), (1,)), ((), ())), preferred_element_type=F32)


def dot_over_rows(a, b):
    return lax.dot_general(a, b, (((0,), (0,)), ((), ())), preferred_element_type=F32)


def factor_block(work, step):
    base = step * BLOCK
    line = lax.broadcasted_iota(jnp.int32, (BLOCK, 1), 0)
    for e in range(EXPERTS_HERE):
        rows = work[e, base : base + BLOCK, :]
        columns = [
            jnp.broadcast_to(rows[:, base + j : base + j + 1], (BLOCK, RANK)) for j in range(BLOCK)
        ]
        for j in range(BLOCK):
            inverse = lax.rsqrt(columns[j][j : j + 1, :])
            scaled = columns[j] * inverse
            below = jnp.where(line > j, scaled, 0.0)
            pivot_row = rows[j : j + 1, :] * jnp.concatenate([inverse, inverse], axis=1)
            below_wide = jnp.concatenate([below, below], axis=1)
            rows = jnp.where(line == j, pivot_row, rows - below_wide * pivot_row)
            for k in range(j + 1, BLOCK):
                columns[k] = columns[k] - below * scaled[k : k + 1, :]
        work[e, base : base + BLOCK, :] = rows
        done = base + BLOCK
        if done < RANK:
            upper = rows[:, :RANK]
            h = upper.astype(BF16).astype(F32)
            m = (upper - h).astype(BF16).astype(F32)
            l = upper - h - m
            hw = rows.astype(BF16).astype(F32)
            mw = (rows - hw).astype(BF16).astype(F32)
            lw = rows - hw - mw
            one = jnp.concatenate([h, h, m, h, m, l], axis=0).astype(BF16)
            two = jnp.concatenate([hw, mw, hw, lw, mw, hw], axis=0).astype(BF16)
            change = dot_over_rows(one, two)
            work[e, done:, :] = work[e, done:, :] - change[done:, :]


def stacked(inverse):
    high, low = split(jnp.transpose(inverse))
    wide = jnp.concatenate([high, low], axis=1)
    return jnp.concatenate([wide, wide], axis=0)


def times(value, stack):
    high, low = split(value)
    both = dot(jnp.concatenate([high, low], axis=1), stack)
    return both[:, :RANK] + both[:, RANK:]


def exponent_of(peak):
    peak = jnp.broadcast_to(jnp.maximum(peak, 1e-30), (HEAD, RANK))
    return jnp.ceil(jnp.log2(peak))


def coded(value, exponent):
    scaled = jnp.round(value * jnp.exp2(15.0 - exponent[:1]))
    return jnp.clip(scaled, -32767.0, 32767.0).astype(jnp.int32).astype(CODE)


def code_tile(target, value):
    exponent = exponent_of(jnp.max(jnp.abs(value), axis=0, keepdims=True))
    target[:RANK, :] = coded(value, exponent)
    target[RANK:, :] = exponent.astype(jnp.int32).astype(CODE)


def step_of(head):
    return jnp.exp2(head.astype(jnp.int32).astype(F32)[:1] - 15.0)


def number(code):
    return code.astype(jnp.int32).astype(F32)


def exchange_kernel(
    grad_hbm,
    moment_hbm,
    factor_hbm,
    buffer,
    new_right,
    left_got,
    right_got,
    grad,
    moment,
    factor,
    high_part,
    low_part,
    raw,
    turned,
    cross,
    own_one,
    got_one,
    sums,
    got_two,
    whole,
    wire,
    gram,
    gram_got,
    gram_all,
    work,
    norms,
    left,
    left_send,
    right_send,
    load_sem,
    one_send,
    one_recv,
    two_send,
    two_recv,
    gram_send,
    gram_recv,
    all_send,
    all_recv,
    norm_send,
    norm_recv,
    ag_send,
    ag_recv,
    fan_send,
    fan_recv,
    own_send,
    own_recv,
):
    place = lax.axis_index("fsdp")
    group = lax.axis_index("expert")
    x = lax.rem(place, SIDE)
    y = lax.div(place, SIDE)

    def spot(shift):
        return lax.rem(place + shift, PEERS)

    def at_fsdp(index):
        return {"fsdp": index, "expert": group}

    def at_expert(shift):
        return {"fsdp": place, "expert": lax.rem(group + shift, GROUPS)}

    def shifted(v, d):
        return lax.rem(v + d, SIDE)

    first = (x, y)
    second = (y, x)

    def first_peer(e, index):
        return at_fsdp(y * SIDE + index if e == 0 else index * SIDE + x)

    def second_peer(e, index):
        return at_fsdp(index * SIDE + x if e == 0 else y * SIDE + index)

    def columns_of(e, a, b):
        return b * SIDE + a if e == 0 else a * SIDE + b

    barrier = pltpu.get_barrier_semaphore()
    for d in range(1, PEERS):
        pl.semaphore_signal(barrier, inc=1, device_id=at_fsdp(spot(d)), device_id_type=MESH)
    for d in (1, 4, GROUPS - 1):
        pl.semaphore_signal(barrier, inc=1, device_id=at_expert(d), device_id_type=MESH)

    loads = {}
    for e in range(EXPERTS_HERE):
        copy = pltpu.make_async_copy(factor_hbm.at[e], factor.at[e], load_sem.at[e, 2 * PARTS])
        copy.start()
        loads[e, 2 * PARTS] = copy
        for p in range(PARTS):
            rows = pl.ds(p * PART_ROWS, PART_ROWS)
            for k, (source, target) in enumerate(((grad_hbm, grad), (moment_hbm, moment))):
                copy = pltpu.make_async_copy(
                    source.at[e, rows], target.at[e, rows], load_sem.at[e, 2 * p + k]
                )
                copy.start()
                loads[e, 2 * p + k] = copy

    sends = []
    last = []

    def send(source, target, send_sem, recv_sem, peer):
        copy = pltpu.make_async_remote_copy(
            src_ref=source,
            dst_ref=target,
            send_sem=send_sem,
            recv_sem=recv_sem,
            device_id=peer,
            device_id_type=MESH,
        )
        copy.start()
        sends.append(copy)
        return copy

    def to_all(source, target, send_sem, recv_sem):
        copies = []
        for d in range(1, PEERS):
            peer = spot(d)
            copies.append(
                send(source(peer), target(d), send_sem.at[d - 1], recv_sem.at[d - 1], at_fsdp(peer))
            )
        return copies

    def first_half(e):
        loads[e, 2 * PARTS].wait()
        value = factor[e]
        norm = jnp.sum(value * value, axis=0, keepdims=True)
        high, low = split(value * lax.rsqrt(jnp.maximum(norm, 1e-30)))
        weights = jnp.concatenate([high, low], axis=1)
        for p in range(PARTS):
            loads[e, 2 * p].wait()
            loads[e, 2 * p + 1].wait()
            rows = slice(p * PART_ROWS, (p + 1) * PART_ROWS)
            total = moment[e, rows, :] + grad[e, rows, :].astype(F32)
            buffer[e, rows, :] = total
            bh, bl = split(total)
            for s in range(PEERS):
                high_part[e, s, rows, :] = bh[:, s * RANK : (s + 1) * RANK]
                low_part[e, s, rows, :] = bl[:, s * RANK : (s + 1) * RANK]
            product = dot(jnp.concatenate([bh, bl], axis=0), weights)
            product = product[:PART_ROWS] + product[PART_ROWS:]
            raw[e, rows, :] = product[:, :RANK] + product[:, RANK:]
        lh, ll = split(raw[e])
        th, tl = split(jnp.transpose(raw[e]))
        turned[e] = jnp.concatenate([th, tl], axis=0)
        four = dot(turned[e], jnp.concatenate([lh, ll], axis=1))
        value = four[:RANK, :RANK] + four[:RANK, RANK:] + (four[RANK:, :RANK] + four[RANK:, RANK:])
        for p in range(PEERS):
            gram[p, e] = value[p * BLOCK : (p + 1) * BLOCK, :]

    def cross_of(e, d):
        a = shifted(first[e], d)
        pairs = []
        for b in range(0, SIDE, 2):
            s0, s1 = columns_of(e, a, b), columns_of(e, a, b + 1)
            bh = jnp.concatenate([high_part[e, s0], high_part[e, s1]], axis=1)
            bl = jnp.concatenate([low_part[e, s0], low_part[e, s1]], axis=1)
            value = dot(turned[e], bh) + dot(turned[e], bl)
            pairs.append(value[:RANK] + value[RANK:])
        if d == 0:
            for b in range(SIDE):
                own_one[e, b] = pairs[b // 2][:, (b % 2) * RANK : (b % 2 + 1) * RANK]
            return
        peak = jnp.maximum(
            *[jnp.max(jnp.abs(value), axis=0, keepdims=True) for value in pairs]
        )
        exponent = exponent_of(jnp.maximum(peak[:, :RANK], peak[:, RANK:]))
        for b in range(SIDE):
            value = pairs[b // 2][:, (b % 2) * RANK : (b % 2 + 1) * RANK]
            cross[e, d - 1, b * RANK : (b + 1) * RANK, :] = coded(value, exponent)
        cross[e, d - 1, SIDE * RANK :, :] = exponent.astype(jnp.int32).astype(CODE)

    def send_one(e, d):
        return send(
            cross.at[e, d - 1],
            got_one.at[e, d - 1],
            one_send.at[e, d - 1],
            one_recv.at[e, d - 1],
            first_peer(e, shifted(first[e], d)),
        )

    def sum_one(e):
        for copy in stage_one[e]:
            copy.wait_recv()
        steps = [step_of(got_one[e, k, SIDE * RANK :, :]) for k in range(SIDE - 1)]
        copies = []
        for d in (2, 1, 3, 0):
            b = shifted(second[e], d)
            rows = pl.ds(pl.multiple_of(b * RANK, RANK), RANK)
            value = own_one[e, b]
            for k in range(SIDE - 1):
                value = value + number(got_one[e, k, rows, :]) * steps[k]
            if d == 0:
                whole[e] = value
                continue
            code_tile(sums.at[e, d - 1], value)
            copies.append(
                send(
                    sums.at[e, d - 1],
                    got_two.at[e, d - 1],
                    two_send.at[e, d - 1],
                    two_recv.at[e, d - 1],
                    second_peer(e, b),
                )
            )
        return copies

    def fan_out(e, b, k):
        for d in (2, 1, 3):
            tile = wire.at[e, first[e], b]
            copy = send(
                tile,
                tile,
                fan_send.at[e, k, d - 1],
                fan_recv.at[e, k, d - 1],
                first_peer(e, shifted(first[e], d)),
            )
            fans[e, k, d] = copy

    def sum_two(e):
        for copy in stage_two[e]:
            copy.wait_recv()
        value = whole[e]
        for k in range(SIDE - 1):
            value = value + number(got_two[e, k, :RANK, :]) * step_of(got_two[e, k, RANK:, :])
        value = jnp.transpose(value)
        whole[e] = value
        mine = second[e]
        tile = wire.at[e, first[e], mine]
        code_tile(tile, value)
        for d in (2, 1, 3):
            around[e, d] = send(
                tile,
                tile,
                ag_send.at[e, d - 1],
                ag_recv.at[e, d - 1],
                second_peer(e, shifted(mine, d)),
            )
        fan_out(e, mine, 0)

    def forward(e):
        for d in (1, 3, 2):
            around[e, d].wait_recv()
            fan_out(e, shifted(second[e], SIDE - d), d)

    stage_one = {}
    stage_two = {}
    around = {}
    fans = {}

    first_half(0)
    for d in (2, 1, 3):
        cross_of(0, d)
    pl.semaphore_wait(barrier, PEERS - 1 + 3)
    stage_one[0] = [send_one(0, d) for d in (2, 1, 3)]
    first_half(1)
    gram_copies = to_all(lambda p: gram.at[p], lambda d: gram_got.at[d - 1], gram_send, gram_recv)
    stage_one[1] = []
    for d in (2, 1, 3):
        cross_of(1, d)
        stage_one[1].append(send_one(1, d))
    cross_of(0, 0)
    cross_of(1, 0)

    for copy in gram_copies:
        copy.wait_recv()
    total = gram[place]
    for d in range(1, PEERS):
        total = total + gram_got[d - 1]
    gram_all[place] = total
    all_copies = to_all(
        lambda p: gram_all.at[place], lambda d: gram_all.at[place], all_send, all_recv
    )
    stage_two[0] = sum_one(0)
    for copy in all_copies:
        copy.wait_recv()

    eye = (
        lax.broadcasted_iota(jnp.int32, (RANK, RANK), 0)
        == lax.broadcasted_iota(jnp.int32, (RANK, RANK), 1)
    ).astype(F32)
    for e in range(EXPERTS_HERE):
        for p in range(PEERS):
            work[e, p * BLOCK : (p + 1) * BLOCK, :RANK] = gram_all[p, e]
        work[e, :, RANK:] = eye
    for step in range(RANK // BLOCK):
        factor_block(work, step)
        if step == 4:
            stage_two[1] = sum_one(1)
        if step == 8:
            sum_two(0)
        if step == 13:
            sum_two(1)

    stacks = [stacked(work[e, :, RANK:]) for e in range(EXPERTS_HERE)]

    norms[place] = jnp.zeros((8, RANK), F32)
    rights = []
    for e in range(EXPERTS_HERE):
        right = times(whole[e], stacks[e])
        rights.append(right)
        norms[place, e : e + 1, :] = jnp.sum(right * right, axis=0, keepdims=True)
    norm_copies = to_all(lambda p: norms.at[place], lambda d: norms.at[place], norm_send, norm_recv)
    forward(0)
    forward(1)

    owners = (1, 4)
    for e in range(EXPERTS_HERE):
        value = times(raw[e], stacks[e])
        left[e] = value.astype(BF16)
        left_send[e] = (value * math.sqrt(D)).astype(BF16)
        last.append(
            send(
                left_send.at[e],
                left_got.at[e],
                own_send.at[e, 0],
                own_recv.at[e, 0],
                at_expert(owners[e]),
            )
        )

    for copy in norm_copies:
        copy.wait_recv()
    squares = norms[0]
    for p in range(1, PEERS):
        squares = squares + norms[p]
    scale = lax.rsqrt(squares * (1.0 / FF) + EPSILON)
    for e in range(EXPERTS_HERE):
        right_send[e] = (rights[e] * scale[e : e + 1, :]).astype(BF16)
        last.append(
            send(
                right_send.at[e],
                right_got.at[e],
                own_send.at[e, 1],
                own_recv.at[e, 1],
                at_expert(owners[e]),
            )
        )

    order = [(0, 0), (1, 0), (3, 0), (2, 0)] + [(k, d) for k in (0, 1, 3, 2) for d in (1, 3, 2)]
    for pair in range(0, PEERS, 2):
        for e in range(EXPERTS_HERE):
            values = []
            for k, d in order[pair : pair + 2]:
                if d:
                    fans[e, k, d].wait_recv()
                a = shifted(first[e], SIDE - d) if d else first[e]
                b = shifted(second[e], SIDE - k) if k else second[e]
                code = wire[e, a, b, :RANK, :]
                values.append(number(code) * step_of(wire[e, a, b, RANK:, :]))
            right = times(jnp.concatenate(values, axis=0), stacks[e])
            part = dot_last(left[e], (right * FEEDBACK).astype(BF16))
            right = right * scale[e : e + 1, :]
            for i, (k, d) in enumerate(order[pair : pair + 2]):
                a = shifted(first[e], SIDE - d) if d else first[e]
                b = shifted(second[e], SIDE - k) if k else second[e]
                span = pl.ds(pl.multiple_of(columns_of(e, a, b) * RANK, RANK), RANK)
                new_right[e, span, :] = right[i * RANK : (i + 1) * RANK]
                buffer[e, :, span] = buffer[e, :, span] - part[:, i * RANK : (i + 1) * RANK]

    for copy in last:
        copy.wait_recv()
    for copy in sends:
        copy.wait_send()


def exchange(gradient, momentum, right_factor):
    dma = pltpu.SemaphoreType.DMA
    vmem = pltpu.VMEM
    n = EXPERTS_HERE
    tile = (RANK, RANK)
    others = SIDE - 1
    return pl.pallas_call(
        exchange_kernel,
        out_shape=(
            vmem((n, ROWS, FF), F32),
            vmem((n, FF, RANK), F32),
            vmem((n, ROWS, RANK), BF16),
            vmem((n, *tile), BF16),
        ),
        in_specs=[pl.BlockSpec(memory_space=pl.ANY)] * 3,
        out_specs=[pl.BlockSpec(memory_space=pltpu.VMEM)] * 4,
        scratch_shapes=[
            vmem((n, ROWS, FF), BF16),
            vmem((n, ROWS, FF), F32),
            vmem((n, FF, RANK), F32),
            vmem((n, PEERS, ROWS, RANK), BF16),
            vmem((n, PEERS, ROWS, RANK), BF16),
            vmem((n, ROWS, RANK), F32),
            vmem((n, 2 * RANK, ROWS), BF16),
            vmem((n, others, CHUNK, RANK), CODE),
            vmem((n, SIDE, *tile), F32),
            vmem((n, others, CHUNK, RANK), CODE),
            vmem((n, others, TILE, RANK), CODE),
            vmem((n, others, TILE, RANK), CODE),
            vmem((n, *tile), F32),
            vmem((n, SIDE, SIDE, TILE, RANK), CODE),
            vmem((PEERS, n, BLOCK, RANK), F32),
            vmem((PEERS - 1, n, BLOCK, RANK), F32),
            vmem((PEERS, n, BLOCK, RANK), F32),
            vmem((n, RANK, 2 * RANK), F32),
            vmem((PEERS, 8, RANK), F32),
            vmem((n, ROWS, RANK), BF16),
            vmem((n, ROWS, RANK), BF16),
            vmem((n, *tile), BF16),
            dma((n, 2 * PARTS + 1)),
            dma((n, others)),
            dma((n, others)),
            dma((n, others)),
            dma((n, others)),
            dma((PEERS - 1,)),
            dma((PEERS - 1,)),
            dma((PEERS - 1,)),
            dma((PEERS - 1,)),
            dma((PEERS - 1,)),
            dma((PEERS - 1,)),
            dma((n, others)),
            dma((n, others)),
            dma((n, SIDE, others)),
            dma((n, SIDE, others)),
            dma((n, 2)),
            dma((n, 2)),
        ],
        compiler_params=pltpu.CompilerParams(
            collective_id=0, has_side_effects=True, vmem_limit_bytes=44 * 2**20
        ),
        cost_estimate=pl.CostEstimate(
            flops=3 * 10**9, bytes_accessed=14 * 10**6, transcendentals=0
        ),
        name="exchange",
    )(gradient, momentum, right_factor)


STORES = 4
STORE_ROWS = ROWS // STORES


def store_kernel(place_ref, new_m, new_r, lgot, rgot, m_out, r_out, left_out, right_out, sem):
    group = lax.axis_index("expert")
    source = EXPERTS_HERE * lax.rem(group + GROUPS - 1, GROUPS)
    straight = place_ref[source] == EXPERTS_HERE * group
    copies = []
    for e in range(EXPERTS_HERE):
        for p in range(STORES):
            rows = pl.ds(p * STORE_ROWS, STORE_ROWS)
            copies.append((new_m.at[e, rows], m_out.at[e, rows]))
        copies.append((new_r.at[e], r_out.at[e]))
    for e in range(EXPERTS_HERE):
        pick = jnp.where(straight, e, 1 - e)
        copies.append((lgot.at[pick], left_out.at[e]))
        copies.append((rgot.at[pick], right_out.at[e]))
    started = []
    for k, (a, b) in enumerate(copies):
        copy = pltpu.make_async_copy(a, b, sem.at[k])
        copy.start()
        started.append(copy)
    for copy in started:
        copy.wait()


def store(placement, pieces):
    n = EXPERTS_HERE
    return pl.pallas_call(
        store_kernel,
        out_shape=(
            jax.ShapeDtypeStruct((n, ROWS, FF), F32),
            jax.ShapeDtypeStruct((n, FF, RANK), F32),
            jax.ShapeDtypeStruct((n, ROWS, RANK), BF16),
            jax.ShapeDtypeStruct((n, RANK, RANK), BF16),
        ),
        in_specs=[pl.BlockSpec(memory_space=pltpu.SMEM)]
        + [pl.BlockSpec(memory_space=pltpu.VMEM)] * 4,
        out_specs=[pl.BlockSpec(memory_space=pl.ANY)] * 4,
        scratch_shapes=[pltpu.SemaphoreType.DMA((n * (STORES + 3),))],
        compiler_params=pltpu.CompilerParams(vmem_limit_bytes=16 * 2**20),
        cost_estimate=pl.CostEstimate(flops=0, bytes_accessed=10 * 10**6, transcendentals=0),
        name="store",
    )(placement, *pieces)


def shards(gradient, momentum, right_factor, placement):
    pieces = exchange(gradient, momentum, right_factor)
    return store(placement, pieces)


def solution(mesh):
    placed = (P("expert", "fsdp", None), P("expert", "fsdp", None), P("expert", None, None), P())
    return jax.shard_map(
        shards,
        mesh=mesh,
        in_specs=placed,
        out_specs=(
            P("expert", "fsdp", None),
            P("expert", None, None),
            P("expert", "fsdp", None),
            P("expert", "fsdp", None),
        ),
        check_vma=False,
    )
```

profile of v0, /device:TPU:0, one launch (start us, length us, event | category | flops | bytes accessed | tf_op | source)
XLA Modules:
  0.0 52.4 jit_solution(13902871059582775697)
XLA Ops:
  0.6 0.0 copy-start
  0.6 47.3 %exchange.1 = (f32[2,448,2048]{2,1,0:T(8,128)S(1)}, f32[2,2048,128]{2,1,0:T(8,128)S(1)}, bf16[2,448,128]{2,1,0:T(8,128)(2,1)S(1)}, bf16[2,128,128]{2,1,0:T(8,128)(2,1)S(1)}) custom-call(bf16[2,448,2048]{2,1,0:T(8,128)(2,1)} %grad_hbm.1, f32[2,448,2048]{2,1,0:T(8,128)} %moment_hbm.1, f32[2,2048,128]{2,1,0:T(8,128)} %factor_hbm.1), custom_call_target="tpu_custom_call" | custom-call | flops 3000000000 | bytes 14000000 | tf_op jit(solution)/shard_map/exchange/pallas_call | solution.py:491
  47.9 0.0 copy-done
  47.9 4.3 %store.1 = (f32[2,448,2048]{2,1,0:T(8,128)}, f32[2,2048,128]{2,1,0:T(8,128)}, bf16[2,448,128]{2,1,0:T(8,128)(2,1)}, bf16[2,128,128]{2,1,0:T(8,128)(2,1)}) custom-call(s32[16]{0:T(128)S(1)} %copy-done, f32[2,448,2048]{2,1,0:T(8,128)S(1)} %get-tuple-element.8.new_m, f32[2,2048,128]{2,1,0:T(8,128)S(1)} %get-tuple-element.9.new_r, ...), custom_call_target="tpu_custom_call" | custom-call | bytes 10000000 | tf_op jit(solution)/shard_map/store/pallas_call | solution.py:581
Async XLA Ops:
  0.6 47.3 %copy-start = (s32[16]{0:T(128)S(1)}, s32[16]{0:T(128)}, u32[]{:S(2)}) copy-start(s32[16]{0:T(128)} %place_ref.1) | copy-start | bytes 196
where the time goes:
time: 52.5 us; the launch traced here: 52.4 us
  Pallas kernels  51.6 us (98%)
  between operations  0.82 us (2%)
    pallas_call x1, Pallas kernels, exchange(): pl.pallas_call(exchange_kernel, out_shape=(vmem((n, ROWS, FF), F32), vmem...  47.3 us
    pallas_call x1, Pallas kernels, store(): pl.pallas_call(store_kernel, out_shape=(jax.ShapeDtypeStruct((n, ROWS, FF...  4.33 us

commit v1 on v0

--- a/solution.py
+++ b/solution.py
@@ -25,6 +25,8 @@
 HEAD = 16
 TILE = RANK + HEAD
 CHUNK = SIDE * RANK + HEAD
+ORDER = (2, 1, 3, 0)
+QUARTER = RANK // SIDE
 MESH = pl.DeviceIdType.MESH
 F32 = jnp.float32
 BF16 = jnp.bfloat16
@@ -140,10 +142,11 @@
     whole,
     wire,
     gram,
-    gram_got,
+    gram_one,
+    gram_two,
     gram_all,
     work,
-    norms,
+    squares,
     left,
     left_send,
     right_send,
@@ -154,10 +157,6 @@
     two_recv,
     gram_send,
     gram_recv,
-    all_send,
-    all_recv,
-    norm_send,
-    norm_recv,
     ag_send,
     ag_recv,
     fan_send,
@@ -170,11 +169,11 @@
     x = lax.rem(place, SIDE)
     y = lax.div(place, SIDE)
 
-    def spot(shift):
-        return lax.rem(place + shift, PEERS)
-
-    def at_fsdp(index):
-        return {"fsdp": index, "expert": group}
+    def along_x(index):
+        return {"fsdp": y * SIDE + index, "expert": group}
+
+    def along_y(index):
+        return {"fsdp": index * SIDE + x, "expert": group}
 
     def at_expert(shift):
         return {"fsdp": place, "expert": lax.rem(group + shift, GROUPS)}
@@ -186,33 +185,40 @@
     second = (y, x)
 
     def first_peer(e, index):
-        return at_fsdp(y * SIDE + index if e == 0 else index * SIDE + x)
+        return along_x(index) if e == 0 else along_y(index)
 
     def second_peer(e, index):
-        return at_fsdp(index * SIDE + x if e == 0 else y * SIDE + index)
+        return along_y(index) if e == 0 else along_x(index)
 
     def columns_of(e, a, b):
         return b * SIDE + a if e == 0 else a * SIDE + b
 
     barrier = pltpu.get_barrier_semaphore()
-    for d in range(1, PEERS):
-        pl.semaphore_signal(barrier, inc=1, device_id=at_fsdp(spot(d)), device_id_type=MESH)
+    for d in range(1, SIDE):
+        for peer in (along_x(shifted(x, d)), along_y(shifted(y, d))):
+            pl.semaphore_signal(barrier, inc=1, device_id=peer, device_id_type=MESH)
     for d in (1, 4, GROUPS - 1):
         pl.semaphore_signal(barrier, inc=1, device_id=at_expert(d), device_id_type=MESH)
 
     loads = {}
-    for e in range(EXPERTS_HERE):
-        copy = pltpu.make_async_copy(factor_hbm.at[e], factor.at[e], load_sem.at[e, 2 * PARTS])
-        copy.start()
-        loads[e, 2 * PARTS] = copy
-        for p in range(PARTS):
+
+    def load(e, p):
+        if p == PARTS:
+            pieces = ((factor_hbm.at[e], factor.at[e]),)
+        else:
             rows = pl.ds(p * PART_ROWS, PART_ROWS)
-            for k, (source, target) in enumerate(((grad_hbm, grad), (moment_hbm, moment))):
-                copy = pltpu.make_async_copy(
-                    source.at[e, rows], target.at[e, rows], load_sem.at[e, 2 * p + k]
-                )
-                copy.start()
-                loads[e, 2 * p + k] = copy
+            pieces = (
+                (grad_hbm.at[e, rows], grad.at[e, rows]),
+                (moment_hbm.at[e, rows], moment.at[e, rows]),
+            )
+        for k, (source, target) in enumerate(pieces):
+            copy = pltpu.make_async_copy(source, target, load_sem.at[e, 2 * p + k])
+            copy.start()
+            loads[e, 2 * p + k] = copy
+
+    load(0, PARTS)
+    for p in range(PARTS):
+        load(0, p)
 
     sends = []
     last = []
@@ -230,17 +236,31 @@
         sends.append(copy)
         return copy
 
-    def to_all(source, target, send_sem, recv_sem):
-        copies = []
-        for d in range(1, PEERS):
-            peer = spot(d)
-            copies.append(
-                send(source(peer), target(d), send_sem.at[d - 1], recv_sem.at[d - 1], at_fsdp(peer))
+    def total_of(slots):
+        return (slots(0) + slots(1)) + (slots(2) + slots(3))
+
+    def to_column(source, target, send_sems, recv_sems):
+        return [
+            send(
+                source(shifted(y, d)),
+                target,
+                send_sems.at[d - 1],
+                recv_sems.at[d - 1],
+                along_y(shifted(y, d)),
             )
-        return copies
+            for d in (2, 1, 3)
+        ]
+
+    def to_row(slot, send_sems, recv_sems):
+        return [
+            send(slot, slot, send_sems.at[d - 1], recv_sems.at[d - 1], along_x(shifted(x, d)))
+            for d in (2, 1, 3)
+        ]
 
     def first_half(e):
         loads[e, 2 * PARTS].wait()
+        if e == 0:
+            load(1, PARTS)
         value = factor[e]
         norm = jnp.sum(value * value, axis=0, keepdims=True)
         high, low = split(value * lax.rsqrt(jnp.maximum(norm, 1e-30)))
@@ -248,6 +268,8 @@
         for p in range(PARTS):
             loads[e, 2 * p].wait()
             loads[e, 2 * p + 1].wait()
+            if e == 0:
+                load(1, p)
             rows = slice(p * PART_ROWS, (p + 1) * PART_ROWS)
             total = moment[e, rows, :] + grad[e, rows, :].astype(F32)
             buffer[e, rows, :] = total
@@ -255,73 +277,68 @@
             for s in range(PEERS):
                 high_part[e, s, rows, :] = bh[:, s * RANK : (s + 1) * RANK]
                 low_part[e, s, rows, :] = bl[:, s * RANK : (s + 1) * RANK]
-            product = dot(jnp.concatenate([bh, bl], axis=0), weights)
-            product = product[:PART_ROWS] + product[PART_ROWS:]
-            raw[e, rows, :] = product[:, :RANK] + product[:, RANK:]
+            product = dot(bh, weights)
+            raw[e, rows, :] = product[:, :RANK] + (product[:, RANK:] + dot(bl, high))
         lh, ll = split(raw[e])
         th, tl = split(jnp.transpose(raw[e]))
         turned[e] = jnp.concatenate([th, tl], axis=0)
         four = dot(turned[e], jnp.concatenate([lh, ll], axis=1))
         value = four[:RANK, :RANK] + four[:RANK, RANK:] + (four[RANK:, :RANK] + four[RANK:, RANK:])
-        for p in range(PEERS):
-            gram[p, e] = value[p * BLOCK : (p + 1) * BLOCK, :]
+        for q in range(SIDE):
+            gram[q, e] = value[q * QUARTER : (q + 1) * QUARTER, :]
 
     def cross_of(e, d):
         a = shifted(first[e], d)
         pairs = []
-        for b in range(0, SIDE, 2):
-            s0, s1 = columns_of(e, a, b), columns_of(e, a, b + 1)
+        for k0, k1 in ((ORDER[0], ORDER[1]), (ORDER[2], ORDER[3])):
+            s0 = columns_of(e, a, shifted(second[e], k0))
+            s1 = columns_of(e, a, shifted(second[e], k1))
             bh = jnp.concatenate([high_part[e, s0], high_part[e, s1]], axis=1)
             bl = jnp.concatenate([low_part[e, s0], low_part[e, s1]], axis=1)
-            value = dot(turned[e], bh) + dot(turned[e], bl)
-            pairs.append(value[:RANK] + value[RANK:])
+            value = dot(turned[e], bh)
+            pairs.append(value[:RANK] + (value[RANK:] + dot(turned[e, :RANK, :], bl)))
+        tiles = [pairs[g // 2][:, (g % 2) * RANK : (g % 2 + 1) * RANK] for g in range(SIDE)]
         if d == 0:
-            for b in range(SIDE):
-                own_one[e, b] = pairs[b // 2][:, (b % 2) * RANK : (b % 2 + 1) * RANK]
+            for g in range(SIDE):
+                own_one[e, g] = tiles[g]
             return
-        peak = jnp.maximum(
-            *[jnp.max(jnp.abs(value), axis=0, keepdims=True) for value in pairs]
+        peak = jnp.maximum(*[jnp.max(jnp.abs(value), axis=0, keepdims=True) for value in pairs])
+        exponent = exponent_of(jnp.maximum(peak[:, :RANK], peak[:, RANK:]))
+        cross[e, d - 1, :HEAD, :] = exponent.astype(jnp.int32).astype(CODE)
+        for g in range(SIDE):
+            cross[e, d - 1, HEAD + g * RANK : HEAD + (g + 1) * RANK, :] = coded(tiles[g], exponent)
+
+    def send_one(e):
+        for g in range(SIDE):
+            start, end = (HEAD + g * RANK if g else 0), HEAD + (g + 1) * RANK
+            for d in (2, 1, 3):
+                stage_one[e, g, d] = send(
+                    cross.at[e, d - 1, start:end],
+                    got_one.at[e, d - 1, start:end],
+                    one_send.at[e, g, d - 1],
+                    one_recv.at[e, g, d - 1],
+                    first_peer(e, shifted(first[e], d)),
+                )
+
+    def sum_one(e, g):
+        for d in (2, 1, 3):
+            stage_one[e, g, d].wait_recv()
+        value = own_one[e, g]
+        for k in range(SIDE - 1):
+            step = step_of(got_one[e, k, :HEAD, :])
+            value = value + number(got_one[e, k, HEAD + g * RANK : HEAD + (g + 1) * RANK, :]) * step
+        d = ORDER[g]
+        if d == 0:
+            whole[e] = value
+            return
+        code_tile(sums.at[e, d - 1], value)
+        stage_two[e, d] = send(
+            sums.at[e, d - 1],
+            got_two.at[e, d - 1],
+            two_send.at[e, d - 1],
+            two_recv.at[e, d - 1],
+            second_peer(e, shifted(second[e], d)),
         )
-        exponent = exponent_of(jnp.maximum(peak[:, :RANK], peak[:, RANK:]))
-        for b in range(SIDE):
-            value = pairs[b // 2][:, (b % 2) * RANK : (b % 2 + 1) * RANK]
-            cross[e, d - 1, b * RANK : (b + 1) * RANK, :] = coded(value, exponent)
-        cross[e, d - 1, SIDE * RANK :, :] = exponent.astype(jnp.int32).astype(CODE)
-
-    def send_one(e, d):
-        return send(
-            cross.at[e, d - 1],
-            got_one.at[e, d - 1],
-            one_send.at[e, d - 1],
-            one_recv.at[e, d - 1],
-            first_peer(e, shifted(first[e], d)),
-        )
-
-    def sum_one(e):
-        for copy in stage_one[e]:
-            copy.wait_recv()
-        steps = [step_of(got_one[e, k, SIDE * RANK :, :]) for k in range(SIDE - 1)]
-        copies = []
-        for d in (2, 1, 3, 0):
-            b = shifted(second[e], d)
-            rows = pl.ds(pl.multiple_of(b * RANK, RANK), RANK)
-            value = own_one[e, b]
-            for k in range(SIDE - 1):
-                value = value + number(got_one[e, k, rows, :]) * steps[k]
-            if d == 0:
-                whole[e] = value
-                continue
-            code_tile(sums.at[e, d - 1], value)
-            copies.append(
-                send(
-                    sums.at[e, d - 1],
-                    got_two.at[e, d - 1],
-                    two_send.at[e, d - 1],
-                    two_recv.at[e, d - 1],
-                    second_peer(e, b),
-                )
-            )
-        return copies
 
     def fan_out(e, b, k):
         for d in (2, 1, 3):
@@ -336,8 +353,8 @@
             fans[e, k, d] = copy
 
     def sum_two(e):
-        for copy in stage_two[e]:
-            copy.wait_recv()
+        for d in (2, 1, 3):
+            stage_two[e, d].wait_recv()
         value = whole[e]
         for k in range(SIDE - 1):
             value = value + number(got_two[e, k, :RANK, :]) * step_of(got_two[e, k, RANK:, :])
@@ -369,28 +386,37 @@
     first_half(0)
     for d in (2, 1, 3):
         cross_of(0, d)
-    pl.semaphore_wait(barrier, PEERS - 1 + 3)
-    stage_one[0] = [send_one(0, d) for d in (2, 1, 3)]
+    pl.semaphore_wait(barrier, 2 * (SIDE - 1) + 3)
+    send_one(0)
     first_half(1)
-    gram_copies = to_all(lambda p: gram.at[p], lambda d: gram_got.at[d - 1], gram_send, gram_recv)
-    stage_one[1] = []
+    gram_one[y] = gram[y]
+    copies = to_column(lambda i: gram.at[i], gram_one.at[y], gram_send.at[0], gram_recv.at[0])
     for d in (2, 1, 3):
         cross_of(1, d)
-        stage_one[1].append(send_one(1, d))
+    send_one(1)
     cross_of(0, 0)
     cross_of(1, 0)
 
-    for copy in gram_copies:
+    sum_one(0, 0)
+    for copy in copies:
         copy.wait_recv()
-    total = gram[place]
-    for d in range(1, PEERS):
-        total = total + gram_got[d - 1]
-    gram_all[place] = total
-    all_copies = to_all(
-        lambda p: gram_all.at[place], lambda d: gram_all.at[place], all_send, all_recv
+    gram_two[x] = total_of(lambda i: gram_one[i])
+    copies = to_row(gram_two.at[x], gram_send.at[1], gram_recv.at[1])
+    sum_one(0, 1)
+    sum_one(0, 2)
+    sum_one(0, 3)
+    sum_one(1, 0)
+    for copy in copies:
+        copy.wait_recv()
+    gram_all[y] = total_of(lambda i: gram_two[i])
+    copies = to_column(
+        lambda i: gram_all.at[y], gram_all.at[y], gram_send.at[2], gram_recv.at[2]
     )
-    stage_two[0] = sum_one(0)
-    for copy in all_copies:
+    sum_one(1, 1)
+    sum_one(1, 2)
+    sum_one(1, 3)
+    sum_two(0)
+    for copy in copies:
         copy.wait_recv()
 
     eye = (
@@ -398,29 +424,19 @@
         == lax.broadcasted_iota(jnp.int32, (RANK, RANK), 1)
     ).astype(F32)
     for e in range(EXPERTS_HERE):
-        for p in range(PEERS):
-            work[e, p * BLOCK : (p + 1) * BLOCK, :RANK] = gram_all[p, e]
+        for q in range(SIDE):
+            work[e, q * QUARTER : (q + 1) * QUARTER, :RANK] = gram_all[q, e]
         work[e, :, RANK:] = eye
     for step in range(RANK // BLOCK):
         factor_block(work, step)
+        if step == 1:
+            sum_two(1)
         if step == 4:
-            stage_two[1] = sum_one(1)
-        if step == 8:
-            sum_two(0)
-        if step == 13:
-            sum_two(1)
+            forward(0)
+        if step == 12:
+            forward(1)
 
     stacks = [stacked(work[e, :, RANK:]) for e in range(EXPERTS_HERE)]
-
-    norms[place] = jnp.zeros((8, RANK), F32)
-    rights = []
-    for e in range(EXPERTS_HERE):
-        right = times(whole[e], stacks[e])
-        rights.append(right)
-        norms[place, e : e + 1, :] = jnp.sum(right * right, axis=0, keepdims=True)
-    norm_copies = to_all(lambda p: norms.at[place], lambda d: norms.at[place], norm_send, norm_recv)
-    forward(0)
-    forward(1)
 
     owners = (1, 4)
     for e in range(EXPERTS_HERE):
@@ -437,14 +453,32 @@
             )
         )
 
-    for copy in norm_copies:
-        copy.wait_recv()
-    squares = norms[0]
-    for p in range(1, PEERS):
-        squares = squares + norms[p]
-    scale = lax.rsqrt(squares * (1.0 / FF) + EPSILON)
-    for e in range(EXPERTS_HERE):
-        right_send[e] = (rights[e] * scale[e : e + 1, :]).astype(BF16)
+    order = [(k, d) for k in (0, 1, 3, 2) for d in (0, 1, 3, 2)]
+    for e in range(EXPERTS_HERE):
+        for pair in range(0, PEERS, 2):
+            values = []
+            places = []
+            for k, d in order[pair : pair + 2]:
+                if d:
+                    fans[e, k, d].wait_recv()
+                a = shifted(first[e], SIDE - d) if d else first[e]
+                b = shifted(second[e], SIDE - k) if k else second[e]
+                places.append(columns_of(e, a, b))
+                values.append(
+                    number(wire[e, a, b, :RANK, :]) * step_of(wire[e, a, b, RANK:, :])
+                )
+            right = times(jnp.concatenate(values, axis=0), stacks[e])
+            for i, place_of in enumerate(places):
+                tile = right[i * RANK : (i + 1) * RANK]
+                span = pl.ds(pl.multiple_of(place_of * RANK, RANK), RANK)
+                new_right[e, span, :] = tile
+                squares[e, pl.ds(place_of, 1), :] = jnp.sum(tile * tile, axis=0, keepdims=True)
+
+    scales = []
+    for e in range(EXPERTS_HERE):
+        mean = jnp.sum(squares[e], axis=0, keepdims=True) * (1.0 / FF)
+        scales.append(lax.rsqrt(mean + EPSILON))
+        right_send[e] = (times(whole[e], stacks[e]) * scales[e]).astype(BF16)
         last.append(
             send(
                 right_send.at[e],
@@ -455,26 +489,13 @@
             )
         )
 
-    order = [(0, 0), (1, 0), (3, 0), (2, 0)] + [(k, d) for k in (0, 1, 3, 2) for d in (1, 3, 2)]
-    for pair in range(0, PEERS, 2):
-        for e in range(EXPERTS_HERE):
-            values = []
-            for k, d in order[pair : pair + 2]:
-                if d:
-                    fans[e, k, d].wait_recv()
-                a = shifted(first[e], SIDE - d) if d else first[e]
-                b = shifted(second[e], SIDE - k) if k else second[e]
-                code = wire[e, a, b, :RANK, :]
-                values.append(number(code) * step_of(wire[e, a, b, RANK:, :]))
-            right = times(jnp.concatenate(values, axis=0), stacks[e])
+    for e in range(EXPERTS_HERE):
+        for s in range(0, FF, 2 * RANK):
+            span = slice(s, s + 2 * RANK)
+            right = new_right[e, span, :]
             part = dot_last(left[e], (right * FEEDBACK).astype(BF16))
-            right = right * scale[e : e + 1, :]
-            for i, (k, d) in enumerate(order[pair : pair + 2]):
-                a = shifted(first[e], SIDE - d) if d else first[e]
-                b = shifted(second[e], SIDE - k) if k else second[e]
-                span = pl.ds(pl.multiple_of(columns_of(e, a, b) * RANK, RANK), RANK)
-                new_right[e, span, :] = right[i * RANK : (i + 1) * RANK]
-                buffer[e, :, span] = buffer[e, :, span] - part[:, i * RANK : (i + 1) * RANK]
+            buffer[e, :, span] = buffer[e, :, span] - part
+            new_right[e, span, :] = right * scales[e]
 
     for copy in last:
         copy.wait_recv()
@@ -513,25 +534,22 @@
             vmem((n, others, TILE, RANK), CODE),
             vmem((n, *tile), F32),
             vmem((n, SIDE, SIDE, TILE, RANK), CODE),
-            vmem((PEERS, n, BLOCK, RANK), F32),
-            vmem((PEERS - 1, n, BLOCK, RANK), F32),
-            vmem((PEERS, n, BLOCK, RANK), F32),
+            vmem((SIDE, n, QUARTER, RANK), F32),
+            vmem((SIDE, n, QUARTER, RANK), F32),
+            vmem((SIDE, n, QUARTER, RANK), F32),
+            vmem((SIDE, n, QUARTER, RANK), F32),
             vmem((n, RANK, 2 * RANK), F32),
-            vmem((PEERS, 8, RANK), F32),
+            vmem((n, PEERS, RANK), F32),
             vmem((n, ROWS, RANK), BF16),
             vmem((n, ROWS, RANK), BF16),
             vmem((n, *tile), BF16),
             dma((n, 2 * PARTS + 1)),
+            dma((n, SIDE, others)),
+            dma((n, SIDE, others)),
             dma((n, others)),
             dma((n, others)),
-            dma((n, others)),
-            dma((n, others)),
-            dma((PEERS - 1,)),
-            dma((PEERS - 1,)),
-            dma((PEERS - 1,)),
-            dma((PEERS - 1,)),
-            dma((PEERS - 1,)),
-            dma((PEERS - 1,)),
+            dma((3, others)),
+            dma((3, others)),
             dma((n, others)),
             dma((n, others)),
             dma((n, SIDE, others)),

time: 52.5 us -> 46.9 us (0.89)
  Pallas kernels: 51.6 us -> 46.2 us
    pallas_call x1, Pallas kernels: 47.3 us -> 41.8 us  [exchange(): pl.pallas_call(exchange_kernel, out_shape=(vmem((n, ROWS, FF), F32), vmem...]
where the time goes in v1:
time: 46.9 us; the launch traced here: 46.8 us
  Pallas kernels  46.2 us (99%)
  between operations  0.66 us (1%)
    pallas_call x1, Pallas kernels, exchange(): pl.pallas_call(exchange_kernel, out_shape=(vmem((n, ROWS, FF), F32), vmem...  41.8 us
    pallas_call x1, Pallas kernels, store(): pl.pallas_call(store_kernel, out_shape=(jax.ShapeDtypeStruct((n, ROWS, FF...  4.33 us

profile of v1, /device:TPU:0, one launch (start us, length us, event | category | flops | bytes accessed | tf_op | source)
XLA Modules:
  0.0 46.8 jit_solution(12495237959110442570)
XLA Ops:
  0.6 0.0 copy-start
  0.6 41.8 %exchange.1 = (f32[2,448,2048]{2,1,0:T(8,128)S(1)}, f32[2,2048,128]{2,1,0:T(8,128)S(1)}, bf16[2,448,128]{2,1,0:T(8,128)(2,1)S(1)}, bf16[2,128,128]{2,1,0:T(8,128)(2,1)S(1)}) custom-call(bf16[2,448,2048]{2,1,0:T(8,128)(2,1)} %grad_hbm.1, f32[2,448,2048]{2,1,0:T(8,128)} %moment_hbm.1, f32[2,2048,128]{2,1,0:T(8,128)} %factor_hbm.1), custom_call_target="tpu_custom_call" | custom-call | flops 3000000000 | bytes 14000000 | tf_op jit(solution)/shard_map/exchange/pallas_call | solution.py:512
  42.5 0.0 copy-done
  42.5 4.3 %store.1 = (f32[2,448,2048]{2,1,0:T(8,128)}, f32[2,2048,128]{2,1,0:T(8,128)}, bf16[2,448,128]{2,1,0:T(8,128)(2,1)}, bf16[2,128,128]{2,1,0:T(8,128)(2,1)}) custom-call(s32[16]{0:T(128)S(1)} %copy-done, f32[2,448,2048]{2,1,0:T(8,128)S(1)} %get-tuple-element.8.new_m, f32[2,2048,128]{2,1,0:T(8,128)S(1)} %get-tuple-element.9.new_r, ...), custom_call_target="tpu_custom_call" | custom-call | bytes 10000000 | tf_op jit(solution)/shard_map/store/pallas_call | solution.py:599
Async XLA Ops:
  0.6 41.8 %copy-start = (s32[16]{0:T(128)S(1)}, s32[16]{0:T(128)}, u32[]{:S(2)}) copy-start(s32[16]{0:T(128)} %place_ref.1) | copy-start | bytes 196

commit v2 on v1

--- a/solution.py
+++ b/solution.py
@@ -21,7 +21,7 @@
 GROUPS = 8
 PARTS = 2
 PART_ROWS = ROWS // PARTS
-BLOCK = 8
+BLOCK = 16
 HEAD = 16
 TILE = RANK + HEAD
 CHUNK = SIDE * RANK + HEAD
@@ -204,12 +204,12 @@
 
     def load(e, p):
         if p == PARTS:
-            pieces = ((factor_hbm.at[e], factor.at[e]),)
+            pieces = ((factor_hbm.at[1 - e], factor.at[e]),)
         else:
             rows = pl.ds(p * PART_ROWS, PART_ROWS)
             pieces = (
-                (grad_hbm.at[e, rows], grad.at[e, rows]),
-                (moment_hbm.at[e, rows], moment.at[e, rows]),
+                (grad_hbm.at[1 - e, rows], grad.at[e, rows]),
+                (moment_hbm.at[1 - e, rows], moment.at[e, rows]),
             )
         for k, (source, target) in enumerate(pieces):
             copy = pltpu.make_async_copy(source, target, load_sem.at[e, 2 * p + k])
@@ -397,27 +397,32 @@
     cross_of(0, 0)
     cross_of(1, 0)
 
+    def gram_next(stage, copies):
+        for copy in copies:
+            copy.wait_recv()
+        if stage == 1:
+            gram_two[x] = total_of(lambda i: gram_one[i])
+            return to_row(gram_two.at[x], gram_send.at[1], gram_recv.at[1])
+        if stage == 2:
+            gram_all[y] = total_of(lambda i: gram_two[i])
+            return to_column(
+                lambda i: gram_all.at[y], gram_all.at[y], gram_send.at[2], gram_recv.at[2]
+            )
+        return None
+
     sum_one(0, 0)
-    for copy in copies:
-        copy.wait_recv()
-    gram_two[x] = total_of(lambda i: gram_one[i])
-    copies = to_row(gram_two.at[x], gram_send.at[1], gram_recv.at[1])
+    copies = gram_next(1, copies)
     sum_one(0, 1)
     sum_one(0, 2)
     sum_one(0, 3)
     sum_one(1, 0)
-    for copy in copies:
-        copy.wait_recv()
-    gram_all[y] = total_of(lambda i: gram_two[i])
-    copies = to_column(
-        lambda i: gram_all.at[y], gram_all.at[y], gram_send.at[2], gram_recv.at[2]
-    )
+    copies = gram_next(2, copies)
     sum_one(1, 1)
     sum_one(1, 2)
     sum_one(1, 3)
     sum_two(0)
-    for copy in copies:
-        copy.wait_recv()
+    sum_two(1)
+    copies = gram_next(3, copies)
 
     eye = (
         lax.broadcasted_iota(jnp.int32, (RANK, RANK), 0)
@@ -430,15 +435,13 @@
     for step in range(RANK // BLOCK):
         factor_block(work, step)
         if step == 1:
-            sum_two(1)
-        if step == 4:
             forward(0)
-        if step == 12:
+        if step == 5:
             forward(1)
 
     stacks = [stacked(work[e, :, RANK:]) for e in range(EXPERTS_HERE)]
 
-    owners = (1, 4)
+    owners = (4, 1)
     for e in range(EXPERTS_HERE):
         value = times(raw[e], stacks[e])
         left[e] = value.astype(BF16)
@@ -454,6 +457,7 @@
         )
 
     order = [(k, d) for k in (0, 1, 3, 2) for d in (0, 1, 3, 2)]
+    scales = {}
     for e in range(EXPERTS_HERE):
         for pair in range(0, PEERS, 2):
             values = []
@@ -474,10 +478,8 @@
                 new_right[e, span, :] = tile
                 squares[e, pl.ds(place_of, 1), :] = jnp.sum(tile * tile, axis=0, keepdims=True)
 
-    scales = []
-    for e in range(EXPERTS_HERE):
         mean = jnp.sum(squares[e], axis=0, keepdims=True) * (1.0 / FF)
-        scales.append(lax.rsqrt(mean + EPSILON))
+        scales[e] = lax.rsqrt(mean + EPSILON)
         right_send[e] = (times(whole[e], stacks[e]) * scales[e]).astype(BF16)
         last.append(
             send(
@@ -497,10 +499,10 @@
             buffer[e, :, span] = buffer[e, :, span] - part
             new_right[e, span, :] = right * scales[e]
 
+    for copy in sends:
+        copy.wait_send()
     for copy in last:
         copy.wait_recv()
-    for copy in sends:
-        copy.wait_send()
 
 
 def exchange(gradient, momentum, right_factor):
@@ -579,10 +581,10 @@
     for e in range(EXPERTS_HERE):
         for p in range(STORES):
             rows = pl.ds(p * STORE_ROWS, STORE_ROWS)
-            copies.append((new_m.at[e, rows], m_out.at[e, rows]))
-        copies.append((new_r.at[e], r_out.at[e]))
+            copies.append((new_m.at[1 - e, rows], m_out.at[e, rows]))
+        copies.append((new_r.at[1 - e], r_out.at[e]))
     for e in range(EXPERTS_HERE):
-        pick = jnp.where(straight, e, 1 - e)
+        pick = jnp.where(straight, 1 - e, e)
         copies.append((lgot.at[pick], left_out.at[e]))
         copies.append((rgot.at[pick], right_out.at[e]))
     started = []

time: 46.9 us -> 44.3 us (0.945)
  Pallas kernels: 46.2 us -> 43.6 us
    pallas_call x1, Pallas kernels: 41.8 us -> 39.3 us  [exchange(): pl.pallas_call(exchange_kernel, out_shape=(vmem((n, ROWS, FF), F32), vmem...]
where the time goes in v2:
time: 44.3 us; the launch traced here: 44.2 us
  Pallas kernels  43.6 us (98%)
  between operations  0.66 us (1%)
    pallas_call x1, Pallas kernels, exchange(): pl.pallas_call(exchange_kernel, out_shape=(vmem((n, ROWS, FF), F32), vmem...  39.3 us
    pallas_call x1, Pallas kernels, store(): pl.pallas_call(store_kernel, out_shape=(jax.ShapeDtypeStruct((n, ROWS, FF...  4.33 us

profile of v2, /device:TPU:0, one launch (start us, length us, event | category | flops | bytes accessed | tf_op | source)
XLA Modules:
  0.0 44.2 jit_solution(9080030907492064997)
XLA Ops:
  0.6 0.0 copy-start
  0.6 39.3 %exchange.1 = (f32[2,448,2048]{2,1,0:T(8,128)S(1)}, f32[2,2048,128]{2,1,0:T(8,128)S(1)}, bf16[2,448,128]{2,1,0:T(8,128)(2,1)S(1)}, bf16[2,128,128]{2,1,0:T(8,128)(2,1)S(1)}) custom-call(bf16[2,448,2048]{2,1,0:T(8,128)(2,1)} %grad_hbm.1, f32[2,448,2048]{2,1,0:T(8,128)} %moment_hbm.1, f32[2,2048,128]{2,1,0:T(8,128)} %factor_hbm.1), custom_call_target="tpu_custom_call" | custom-call | flops 3000000000 | bytes 14000000 | tf_op jit(solution)/shard_map/exchange/pallas_call | solution.py:514
  39.9 0.0 copy-done
  39.9 4.3 %store.1 = (f32[2,448,2048]{2,1,0:T(8,128)}, f32[2,2048,128]{2,1,0:T(8,128)}, bf16[2,448,128]{2,1,0:T(8,128)(2,1)}, bf16[2,128,128]{2,1,0:T(8,128)(2,1)}) custom-call(s32[16]{0:T(128)S(1)} %copy-done, f32[2,448,2048]{2,1,0:T(8,128)S(1)} %get-tuple-element.8.new_m, f32[2,2048,128]{2,1,0:T(8,128)S(1)} %get-tuple-element.9.new_r, ...), custom_call_target="tpu_custom_call" | custom-call | bytes 10000000 | tf_op jit(solution)/shard_map/store/pallas_call | solution.py:601
Async XLA Ops:
  0.6 39.3 %copy-start = (s32[16]{0:T(128)S(1)}, s32[16]{0:T(128)}, u32[]{:S(2)}) copy-start(s32[16]{0:T(128)} %place_ref.1) | copy-start | bytes 196
